TPU v7x, 32 devices: a whole 2x2x4 slice. The times are simulated.
32 devices in a mesh: train: 2 (over y), replica: 4 (over x, core), ep: 4 (over z).
Axes of the slice: x: 2, y: 2, z: 4, core: 2. Of those that a mesh axis runs over, the one named last changes fastest.
Arguments:
- master: float32 [8, 2048, 7168], P('ep', 'replica', 'train'), may hold values from -6 to 6
- gradient: bfloat16 [8, 2048, 7168], P('ep', 'replica', 'train'), may hold values from -1000 to 1000
- second: float32 [8, 2048, 7168], P('ep', 'replica', 'train'), may hold values from 0.1 to 2
- placement: int32 [4, 8], replicated, may hold values from 0 to 3, as said below
Outputs:
- master_new: float32 [8, 2048, 7168], P('ep', 'replica', 'train')
- second_new: float32 [8, 2048, 7168], P('ep', 'replica', 'train')
- quantized: bfloat16 [4, 4, 2, 2048, 7168], P('replica', 'ep', None, None, 'train')
- scales: float32 [4, 4, 2, 16, 56], P('replica', 'ep', None, None, 'train')
Inputs may be any that keep to these rules, and one draw needn't show every extreme that they name: `placement`: in each row every ep index is named by exactly 2 experts.
All inputs are finite; a program needn't handle non-finite values. Where the computation divides by a largest or mean magnitude, that divisor is 1e-20 or more.
Results may differ from a plain program's by a relative error of at most 0.006.
Values may be sent and summed in bfloat16 or wider, within the bound.
A program may use at most 320 MiB of HBM per device.

v0:
```python
import jax
import jax.numpy as jnp
from jax import lax
from jax.sharding import PartitionSpec as P

BLOCK = 128


decay_rate = 0.95
step_size = 0.3


def block_quantize(values):
    full_shape = values.shape
    blocks = values.astype(jnp.float32).reshape(
        full_shape[:-2] + (full_shape[-2] // BLOCK, BLOCK, full_shape[-1] // BLOCK, BLOCK)
    )
    largest = jnp.max(jnp.abs(blocks), axis=(-3, -1)) + 1e-06
    scaled = (blocks / largest[..., :, None, :, None]).astype(jnp.bfloat16).reshape(full_shape)
    return (scaled, largest)


def slot_table(placement, holders, per_device):
    matches = (placement[:, None, :] == jnp.arange(holders, dtype=jnp.int32)[None, :, None]).astype(
        jnp.int32
    )
    rank_within = jnp.cumsum(matches, axis=-1) - 1
    expert_ids = jnp.arange(placement.shape[-1], dtype=jnp.int32)
    slot_numbers = jnp.arange(per_device, dtype=jnp.int32)
    selected = matches[..., None, :] * (rank_within[..., None, :] == slot_numbers[:, None]).astype(
        jnp.int32
    )
    return jnp.sum(selected * expert_ids, axis=-1)


def body(master, gradient, second, placement):
    values = gradient.astype(jnp.float32)
    square_sum = lax.psum(jnp.sum(values * values), ("train", "replica", "ep"))
    n_train = lax.axis_size("train")
    n_replica = lax.axis_size("replica")
    n_holders = lax.axis_size("ep")
    root_mean = jnp.sqrt(square_sum / (values.size * n_train * n_replica * n_holders) + 1e-06)
    clipped = values / root_mean
    second_new = decay_rate * second + (1.0 - decay_rate) * clipped * clipped
    master_new = master - step_size * clipped / (jnp.sqrt(second_new) + 1e-08)
    weights = master_new.astype(jnp.bfloat16)
    per_device, row_count, col_count = weights.shape
    slot_experts = slot_table(placement, n_holders, per_device)
    replica_index = lax.axis_index("replica")
    holder_index = lax.axis_index("ep")
    own_slots = slot_experts[replica_index, holder_index]
    initial = jnp.zeros((per_device, n_replica * row_count, col_count), jnp.bfloat16)
    pieces = lax.all_gather(weights[None], ("replica", "ep"), axis=0, tiled=True)

    def place_piece(piece_index, current):
        source_replica = piece_index // n_holders
        source_holder = piece_index % n_holders
        arriving = lax.dynamic_index_in_dim(pieces, piece_index, 0, False)
        for slot_index in range(per_device):
            expert_id = own_slots[slot_index]
            chosen = lax.dynamic_index_in_dim(arriving, expert_id % per_device, 0, False)
            corner = (jnp.int32(slot_index), source_replica * row_count, jnp.int32(0))
            existing = lax.dynamic_slice(current, corner, (1, row_count, col_count))[0]
            updated = jnp.where(expert_id // per_device == source_holder, chosen, existing)
            current = lax.dynamic_update_slice(current, updated[None], corner)
        return current

    gathered = lax.fori_loop(0, pieces.shape[0], place_piece, initial)
    scaled, largest = block_quantize(gathered)
    return (master_new, second_new, scaled[None, None], largest[None, None])


def solution(mesh):
    return jax.shard_map(
        body,
        mesh=mesh,
        in_specs=(
            P("ep", "replica", "train"),
            P("ep", "replica", "train"),
            P("ep", "replica", "train"),
            P(),
        ),
        out_specs=(
            P("ep", "replica", "train"),
            P("ep", "replica", "train"),
            P("replica", "ep", None, None, "train"),
            P("replica", "ep", None, None, "train"),
        ),
        check_vma=False,
    )
```

profile of v0, /device:TPU:0, one launch (start us, length us, event | category | flops | bytes accessed | tf_op | source)
XLA Modules:
  0.0 1165.8 jit_solution(10882504617263550309)
XLA Ops:
  7.2 0.0 all-gather.3.cloned.1.call-start
  7.2 7.5 fusion.4
  14.7 42.4 %psum.7 = f32[]{:T(128)} all-reduce(f32[]{:T(128)} %fusion.4), channel_id=1, replica_groups=mesh['train'=2,'replica'=4,'ep'=4] {'train','replica','ep'}, use_global_device_ids=true, to_apply=%region_1.0 | all-reduce | flops 1 | bytes 8 | tf_op jit(solution)/shard_map/psum | solution.py:38
  57.7 0.0 copy-start
  57.7 25.6 %fusion.8 = (bf16[2,512,3584]{2,1,0:T(8,128)(2,1)}, f32[2,512,3584]{2,1,0:T(8,128)}, f32[2,512,3584]{2,1,0:T(8,128)}) fusion(f32[2,512,3584]{2,1,0:T(8,128)} %param.6, f32[]{:T(128)S(6)} %sqrt.6, bf16[2,512,3584]{2,1,0:T(8,128)(2,1)} %param.7, f32[2,512,3584]{2,1,0:T(8,128)} %param.8), kind=kLoop, calls=%fused_computation.22 | loop fusion | flops 40370176 | bytes 73400320 | tf_op jit(solution)/shard_map/convert_element_type | solution.py:46
  83.3 0.0 all-gather.3.cloned.1.call-update
  83.4 0.0 copy-done
  83.4 0.7 reduce_window_sum.11
  84.1 0.2 multiply_reduce_fusion
  84.3 0.1 constant_dynamic-slice_fusion
  84.4 0.6 fusion.10
  90.4 592.4 %all-gather.3.cloned.1.call-done = bf16[32,512,3584]{2,1,0:T(8,128)(2,1)} async-done(((bf16[2,512,3584]{2,1,0:T(8,128)(2,1)}), bf16[32,512,3584]{2,1,0:T(8,128)(2,1)}) %all-gather.3.cloned.1.call-update) | async-done | bytes 117440528 | tf_op jit(solution)/shard_map/all_gather | solution.py:53
  682.8 9.8 broadcast_in_dim.8
  692.5 188.1 %while.17 = (s32[]{:T(128)}, bf16[2,2048,3584]{2,1,0:T(8,128)(2,1)}, s32[]{:T(128)}, bf16[16,2,512,3584]{3,2,1,0:T(8,128)(2,1)}, s32[]{:T(128)}, /*index=5*/s32[...) while((s32[]{:T(128)}, ...), condition=%wide.region_5.6_spmd, body=%wide.region_4.5_spmd.sunk | while | flops 3670037 | bytes 22021488 | solution.py:68
  692.5 5.9 fusion.13
  698.4 5.9 fusion.14
  704.3 5.9 fusion.13
  710.2 5.9 fusion.14
  716.1 5.9 fusion.13
  721.9 5.9 fusion.14
  727.8 5.9 fusion.13
  733.7 5.9 fusion.14
  739.6 5.9 fusion.13
  745.5 5.9 fusion.14
  751.3 5.9 fusion.13
  757.2 5.9 fusion.14
  763.1 5.9 fusion.13
  769.0 5.9 fusion.14
  774.8 5.9 fusion.13
  780.7 5.9 fusion.14
  786.6 5.9 fusion.13
  792.5 5.9 fusion.14
  798.4 5.9 fusion.13
  804.2 5.9 fusion.14
  810.1 5.9 fusion.13
  816.0 5.9 fusion.14
  821.9 5.9 fusion.13
  827.8 5.9 fusion.14
  833.6 5.9 fusion.13
  839.5 5.9 fusion.14
  845.4 5.9 fusion.13
  851.3 5.9 fusion.14
  857.2 5.9 fusion.13
  863.0 5.9 fusion.14
  868.9 5.9 fusion.13
  874.8 5.9 fusion.14
  880.7 37.5 %copy.14 = bf16[2,2048,3584]{1,2,0:T(8,128)(2,1)} copy(bf16[2,2048,3584]{2,1,0:T(8,128)(2,1)} %get-tuple-element.463) | data formatting | bytes 58720256 | tf_op jit(solution)/shard_map/while | solution.py:68
  918.2 28.2 %convert_abs_fusion = f32[2,2048,3584]{1,2,0:T(8,128)} fusion(bf16[2,2048,3584]{1,2,0:T(8,128)(2,1)} %copy.14), kind=kLoop, calls=%fused_computation.5 | loop fusion | flops 29360128 | bytes 88080384 | tf_op jit(solution)/shard_map/abs | solution.py:18
  946.4 39.7 %copy.17 = f32[896,8,16,128]{3,2,1,0:T(8,128)} copy(f32[896,8,16,128]{3,1,2,0:T(8,128)} %bitcast.30) | data formatting | bytes 117440512
  986.1 18.4 %reduce_max.9 = f32[2,16,28]{1,2,0:T(8,128)S(1)} reduce(f32[2,16,128,28,128]{2,1,4,3,0:T(8,128)} %bitcast.29, f32[]{:T(128)} %constant.354.clone.1), dimensions={2,4}, to_apply=%region_6.7 | reduce | flops 14679168 | bytes 58723844 | tf_op jit(solution)/shard_map/reduce_max | solution.py:18
  1004.5 0.7 copy.16
  1005.2 18.6 %div.63 = f32[2,16,128,28,128]{2,1,4,3,0:T(8,128)} broadcast(f32[2,16,28]{1,2,0:T(8,128)S(1)} %get-tuple-element.494), dimensions={0,1,3} | broadcast | bytes 58723840 | tf_op jit(solution)/shard_map/div | solution.py:19
  1023.8 61.7 %div.64 = f32[2,2048,3584]{1,2,0:T(8,128)} reshape(f32[2,16,128,28,128]{2,1,4,3,0:T(8,128)} %div.63) | data formatting | bytes 117440512 | tf_op jit(solution)/shard_map/div | solution.py:19
  1085.4 37.6 %fusion.3 = bf16[1,1,2,2048,3584]{3,4,2,1,0:T(8,128)(2,1)} fusion(f32[2,2048,3584]{1,2,0:T(8,128)} %div.64, bf16[2,2048,3584]{1,2,0:T(8,128)(2,1)} %copy.14), kind=kLoop, calls=%fused_computation.7 | loop fusion | flops 44040192 | bytes 117440512 | tf_op jit(solution)/shard_map/convert_element_type | solution.py:19
  1123.0 35.9 %copy.15 = bf16[1,1,2,2048,3584]{4,3,2,1,0:T(8,128)(2,1)} copy(bf16[1,1,2,2048,3584]{3,4,2,1,0:T(8,128)(2,1)} %fusion.3) | data formatting | bytes 58720256
  (3 shorter events, 0.0 us)
Async XLA Ops:
  7.2 675.6 %all-gather.3.cloned.1.call-start = ((), (), s32[]{:S(2)}) async-start(), calls=%async_computation | async-start | bytes 124780544 | tf_op jit(solution)/shard_map/all_gather | solution.py:53
  57.7 25.6 %copy-start = (s32[4,8]{1,0:T(4,128)S(1)}, s32[4,8]{1,0:T(4,128)}, u32[]{:S(2)}) copy-start(s32[4,8]{1,0:T(4,128)} %param.9) | copy-start | bytes 388
Sparse Core Ops, SparseCore 0:
  83.5 599.2 all-gather.2
where the time goes:
time: 1170 us
  waiting for transfers between devices  592 us (51%)
  other arithmetic  306 us (26%)
  local copies, waits for them, and re-layouts  204 us (17%)
  blocking collectives  42.4 us (4%)
  between operations  20.1 us (2%)
    all_gather x1, waiting for transfers between devices, body(): lax.all_gather(weights[None], ('replica', 'ep'), axis=0, tiled=True)  592 us
    dynamic_update_slice x32, other arithmetic, place_piece(): current = lax.dynamic_update_slice(current, updated[None], corner)  188 us
    div x2, local copies, waits for them, and re-layouts, block_quantize(): blocks / largest[..., :, None, :, None]  80.2 us
    unnamed x5, local copies, waits for them, and re-layouts  76.3 us
    psum x1, blocking collectives, body(): square_sum = lax.psum(jnp.sum(values * values), ('train', 'replica', 'ep'))  42.4 us
    convert_element_type x1, other arithmetic, block_quantize(): (blocks / largest[..., :, None, :, None]).astype(jnp.bfloat16)  37.6 us
    while x1, local copies, waits for them, and re-layouts, body(): gathered = lax.fori_loop(0, pieces.shape[0], place_piece, initial)  37.5 us
    abs x1, other arithmetic, block_quantize(): largest = jnp.max(jnp.abs(blocks), axis=(-3, -1)) + 1e-06  28.2 us
  transfers between devices with their start and end apart: 1, of which 1 were waited for; matrix products, arithmetic and copies ran while one was open for 0% of the time, Pallas kernels for 0%

commit v1 on v0

v1 whole, which is shorter than its diff:
```python
import functools

import jax
import jax.numpy as jnp
from jax import lax
from jax.experimental import pallas as pl
from jax.experimental.pallas import tpu as pltpu
from jax.sharding import PartitionSpec as P

BLOCK = 128
HEIGHT = 64
MESH = pl.DeviceIdType.MESH

decay_rate = 0.95
step_size = 0.3


def slot_table(placement, holders, per_device):
    matches = (placement[:, None, :] == jnp.arange(holders, dtype=jnp.int32)[None, :, None]).astype(
        jnp.int32
    )
    rank_within = jnp.cumsum(matches, axis=-1) - 1
    expert_ids = jnp.arange(placement.shape[-1], dtype=jnp.int32)
    slot_numbers = jnp.arange(per_device, dtype=jnp.int32)
    selected = matches[..., None, :] * (rank_within[..., None, :] == slot_numbers[:, None]).astype(
        jnp.int32
    )
    return jnp.sum(selected * expert_ids, axis=-1)


def exchange_kernel(n_rep, n_ep, rounds, table_ref, w_ref, out_ref, *scratch):
    lands = scratch[:rounds]
    stage, own_sem, keep_sem, zrecv, lsend, rsend, xsend, xrecv = scratch[rounds:]
    z = lax.axis_index("ep")
    me = lax.axis_index("replica")
    per, row_count, _ = w_ref.shape
    height = row_count // rounds

    barrier = pltpu.get_barrier_semaphore()
    for step in range(1, n_rep):
        peer = lax.rem(me + step, n_rep)
        pl.semaphore_signal(barrier, inc=1, device_id={"replica": peer}, device_id_type=MESH)

    @pl.when(z > 0)
    def _():
        pl.semaphore_signal(barrier, inc=1, device_id={"ep": z - 1}, device_id_type=MESH)

    @pl.when(z < n_ep - 1)
    def _():
        pl.semaphore_signal(barrier, inc=1, device_id={"ep": z + 1}, device_id_type=MESH)

    def own_copy(t):
        return pltpu.make_async_copy(
            w_ref.at[:, pl.ds(t * height, height), :],
            lands[t].at[pl.ds(per * z, per)],
            own_sem.at[t],
        )

    for t in range(rounds):
        own_copy(t).start()

    lines = jnp.where(z > 0, 1, 0) + jnp.where(z < n_ep - 1, 1, 0)
    pl.semaphore_wait(barrier, n_rep - 1 + lines)

    def line_copy(t, q, to, sems):
        piece = lands[t].at[pl.ds(per * q, per)]
        return pltpu.make_async_remote_copy(
            src_ref=piece,
            dst_ref=piece,
            send_sem=sems.at[t, q],
            recv_sem=zrecv.at[t, q],
            device_id={"ep": to},
            device_id_type=MESH,
        )

    def left(t, q):
        return line_copy(t, q, z - 1, lsend)

    def right(t, q):
        return line_copy(t, q, z + 1, rsend)

    def send_left(t, q):
        @pl.when(z > 0)
        def _():
            left(t, q).start()

    def send_right(t, q):
        @pl.when(z < n_ep - 1)
        def _():
            right(t, q).start()

    def offer(t):
        own_copy(t).wait()
        send_left(t, z)
        send_right(t, z)

    def rows_of(source, t):
        return pl.ds(pl.multiple_of(source * row_count + t * height, height), height)

    def place_copy(t, step):
        return pltpu.make_async_remote_copy(
            src_ref=stage.at[t % 2, step],
            dst_ref=out_ref.at[:, rows_of(me, t), :],
            send_sem=xsend.at[t, step],
            recv_sem=xrecv.at[t, step],
            device_id={"replica": lax.rem(me + step, n_rep)},
            device_id_type=MESH,
        )

    def keep_copy(t):
        return pltpu.make_async_copy(
            stage.at[t % 2, 0], out_ref.at[:, rows_of(me, t), :], keep_sem.at[t]
        )

    def drain(t):
        keep_copy(t).wait()
        for step in range(1, n_rep):
            place_copy(t, step).wait_send()

    offer(0)
    for t in range(rounds):
        if t + 1 < rounds:
            offer(t + 1)
        for d in range(1, n_ep):

            @pl.when(z + d < n_ep)
            def _():
                left(t, z + d).wait_recv()
                send_left(t, z + d)

            @pl.when(z - d >= 0)
            def _():
                right(t, z - d).wait_recv()
                send_right(t, z - d)

        if t >= 2:
            drain(t - 2)
        for step in list(range(1, n_rep)) + [0]:
            dest = lax.rem(me + step, n_rep)
            for k in range(per):
                expert = table_ref[(dest * n_ep + z) * per + k]
                stage[t % 2, step, k] = lands[t][expert]
            if step:
                place_copy(t, step).start()
            else:
                keep_copy(t).start()

    for t in range(max(rounds - 2, 0), rounds):
        drain(t)
    for t in range(rounds):
        for step in range(1, n_rep):
            place_copy(t, step).wait_recv()
        for d in range(n_ep):

            @pl.when(jnp.logical_and(z + d < n_ep, z > 0))
            def _():
                left(t, z + d).wait_send()

            @pl.when(jnp.logical_and(z - d >= 0, z < n_ep - 1))
            def _():
                right(t, z - d).wait_send()


def exchange(table, weights, n_rep, n_ep):
    per, row_count, col_count = weights.shape
    rounds = row_count // HEIGHT
    dma = pltpu.SemaphoreType.DMA
    moved = 2 * per * n_rep * row_count * col_count * 2
    return pl.pallas_call(
        functools.partial(exchange_kernel, n_rep, n_ep, rounds),
        out_shape=jax.ShapeDtypeStruct((per, n_rep * row_count, col_count), weights.dtype),
        in_specs=[
            pl.BlockSpec(memory_space=pltpu.SMEM),
            pl.BlockSpec(memory_space=pl.ANY),
        ],
        out_specs=pl.BlockSpec(memory_space=pl.ANY),
        scratch_shapes=[
            pltpu.VMEM((per * n_ep, HEIGHT, col_count), weights.dtype) for _ in range(rounds)
        ]
        + [
            pltpu.VMEM((2, n_rep, per, HEIGHT, col_count), weights.dtype),
            dma((rounds,)),
            dma((rounds,)),
            dma((rounds, n_ep)),
            dma((rounds, n_ep)),
            dma((rounds, n_ep)),
            dma((rounds, n_rep)),
            dma((rounds, n_rep)),
        ],
        compiler_params=pltpu.CompilerParams(
            collective_id=0, has_side_effects=True, vmem_limit_bytes=52 * 1024 * 1024
        ),
        cost_estimate=pl.CostEstimate(flops=0, bytes_accessed=moved, transcendentals=0),
    )(table, weights)


def scale_kernel(w_ref, out_ref, scale_ref):
    cells = w_ref.shape[2] // BLOCK
    lane = lax.broadcasted_iota(jnp.int32, (1, cells), 1)
    scales = jnp.zeros((1, cells), jnp.float32)
    for cell in range(cells):
        columns = slice(cell * BLOCK, (cell + 1) * BLOCK)
        values = w_ref[0, :, columns].astype(jnp.float32)
        largest = jnp.max(jnp.abs(values), axis=(0, 1), keepdims=True) + 1e-06
        out_ref[0, :, columns] = (values * (1.0 / largest)).astype(out_ref.dtype)
        scales = jnp.where(lane == cell, largest, scales)
    scale_ref[0, 0] = scales


def block_quantize(weights):
    per, row_count, col_count = weights.shape
    strips, cells = row_count // BLOCK, col_count // BLOCK
    scaled, scales = pl.pallas_call(
        scale_kernel,
        grid=(per, strips),
        in_specs=[pl.BlockSpec((1, BLOCK, col_count), lambda k, i: (k, i, 0))],
        out_specs=[
            pl.BlockSpec((1, BLOCK, col_count), lambda k, i: (k, i, 0)),
            pl.BlockSpec((1, 1, 1, cells), lambda k, i: (k, i, 0, 0)),
        ],
        out_shape=[
            jax.ShapeDtypeStruct(weights.shape, weights.dtype),
            jax.ShapeDtypeStruct((per, strips, 1, cells), jnp.float32),
        ],
        compiler_params=pltpu.CompilerParams(vmem_limit_bytes=32 * 1024 * 1024),
    )(weights)
    return scaled, scales[:, :, 0]


def body(master, gradient, second, placement):
    values = gradient.astype(jnp.float32)
    square_sum = lax.psum(jnp.sum(values * values), ("train", "replica", "ep"))
    n_train = lax.axis_size("train")
    n_rep = lax.axis_size("replica")
    n_ep = lax.axis_size("ep")
    root_mean = jnp.sqrt(square_sum / (values.size * n_train * n_rep * n_ep) + 1e-06)
    clipped = values / root_mean
    second_new = decay_rate * second + (1.0 - decay_rate) * clipped * clipped
    master_new = master - step_size * clipped / (jnp.sqrt(second_new) + 1e-08)
    weights = master_new.astype(jnp.bfloat16)
    table = slot_table(placement, n_ep, weights.shape[0]).reshape(-1)
    gathered = exchange(table, weights, n_rep, n_ep)
    scaled, scales = block_quantize(gathered)
    return (master_new, second_new, scaled[None, None], scales[None, None])


def solution(mesh):
    return jax.shard_map(
        body,
        mesh=mesh,
        in_specs=(
            P("ep", "replica", "train"),
            P("ep", "replica", "train"),
            P("ep", "replica", "train"),
            P(),
        ),
        out_specs=(
            P("ep", "replica", "train"),
            P("ep", "replica", "train"),
            P("replica", "ep", None, None, "train"),
            P("replica", "ep", None, None, "train"),
        ),
        check_vma=False,
    )
```

time: 1170 us -> 635 us (0.54)
  waiting for transfers between devices: 592 us -> 0 us
  Pallas kernels: 0 us -> 556 us
  other arithmetic: 306 us -> 34.7 us
  local copies, waits for them, and re-layouts: 204 us -> 0.21 us
  between operations: 20.1 us -> 1.34 us
    all_gather x1 -> x0, waiting for transfers between devices: 592 us -> none  [body(): lax.all_gather(weights[None], ('replica', 'ep'), axis=0, tiled=True)]
    pallas_call x0 -> x2, Pallas kernels: none -> 556 us  [the longest x1 520 us: exchange(): pl.pallas_call(functools.partial(exchange_kernel, n_rep, n_ep, rounds), o...]
    dynamic_update_slice x32 -> x0, other arithmetic: 188 us -> none  [place_piece(): current = lax.dynamic_update_slice(current, updated[None], corner)]
    div x2 -> x0, local copies, waits for them, and re-layouts: 80.2 us -> none  [block_quantize(): blocks / largest[..., :, None, :, None]]
    unnamed x5 -> x0, local copies, waits for them, and re-layouts: 76.3 us -> none
    convert_element_type x1 -> x0, other arithmetic: 37.6 us -> none  [block_quantize(): (blocks / largest[..., :, None, :, None]).astype(jnp.bfloat16)]
    while x1 -> x0, local copies, waits for them, and re-layouts: 37.5 us -> none  [body(): gathered = lax.fori_loop(0, pieces.shape[0], place_piece, initial)]
    abs x1 -> x0, other arithmetic: 28.2 us -> none  [block_quantize(): largest = jnp.max(jnp.abs(blocks), axis=(-3, -1)) + 1e-06]
  transfers between devices with their start and end apart: 1 -> 0, of which waited for: 1 -> 0; matrix products, arithmetic and copies ran while one was open for 0% -> 0% of each run, Pallas kernels for 0% -> 0%
where the time goes in v1:
time: 635 us; the launch traced here: 634 us
  Pallas kernels  556 us (88%)
  blocking collectives  42.2 us (7%)
  other arithmetic  34.7 us (5%)
    pallas_call x1, Pallas kernels, exchange(): pl.pallas_call(functools.partial(exchange_kernel, n_rep, n_ep, rounds), o...  520 us
    psum x1, blocking collectives, body(): square_sum = lax.psum(jnp.sum(values * values), ('train', 'replica', 'ep'))  42.2 us
    pallas_call x1, Pallas kernels, block_quantize(): pl.pallas_call(scale_kernel, grid=(per, strips), in_specs=[pl.BlockSpec((...  36.2 us
    convert_element_type x1, other arithmetic, body(): weights = master_new.astype(jnp.bfloat16)  25.6 us

profile of v1, /device:TPU:0, one launch (start us, length us, event | category | flops | bytes accessed | tf_op | source)
XLA Modules:
  0.0 634.3 jit_solution(13052757143299935340)
XLA Ops:
  0.6 7.5 %fusion = f32[]{:T(128)} fusion(bf16[2,512,3584]{2,1,0:T(8,128)(2,1)} %param.5), kind=kLoop, calls=%fused_computation.3 | loop fusion | flops 11010047 | bytes 7340036 | tf_op jit(solution)/shard_map/reduce_sum | solution.py:232
  8.1 42.2 %psum.7 = f32[]{:T(128)} all-reduce(f32[]{:T(128)} %fusion), channel_id=1, replica_groups=mesh['train'=2,'replica'=4,'ep'=4] {'train','replica','ep'}, use_global_device_ids=true, to_apply=%region_1.0 | all-reduce | flops 1 | bytes 8 | tf_op jit(solution)/shard_map/psum | solution.py:232
  51.0 0.7 fusion.2
  51.7 0.7 reduce_window_sum.11
  52.4 0.2 multiply_reduce_fusion
  52.6 0.1 copy.8
  52.7 0.1 reshape.27.table_ref
  52.8 25.6 %fusion.3 = (bf16[2,512,3584]{2,1,0:T(8,128)(2,1)}, f32[2,512,3584]{2,1,0:T(8,128)}, f32[2,512,3584]{2,1,0:T(8,128)}) fusion(f32[2,512,3584]{2,1,0:T(8,128)} %param.4, f32[]{:T(128)S(6)} %sqrt.6, bf16[2,512,3584]{2,1,0:T(8,128)(2,1)} %param.5, f32[2,512,3584]{2,1,0:T(8,128)} %param.6), kind=kLoop, calls=%fused_computation.11 | loop fusion | flops 40370176 | bytes 73400320 | tf_op jit(solution)/shard_map/convert_element_type | solution.py:240
  78.4 519.7 %shard_map.75.w_ref = bf16[2,2048,3584]{2,1,0:T(8,128)(2,1)} custom-call(s32[32]{0:T(128)S(1)} %reshape.27.table_ref, bf16[2,512,3584]{2,1,0:T(8,128)(2,1)} %get-tuple-element.8.w_ref), custom_call_target="tpu_custom_call" | custom-call | bytes 58720256 | tf_op jit(solution)/shard_map/pallas_call | solution.py:169
  598.1 36.2 %shard_map.76 = (bf16[2,2048,3584]{2,1,0:T(8,128)(2,1)}, f32[2,16,1,28]{3,2,1,0:T(1,128)}) custom-call(bf16[2,2048,3584]{2,1,0:T(8,128)(2,1)} %shard_map.75.w_ref), custom_call_target="tpu_custom_call" | custom-call | tf_op jit(solution)/shard_map/pallas_call | solution.py:213
  (1 shorter events, 0.0 us)

commit v2 on v1

v2 whole, which is shorter than its diff:
```python
import functools

import jax
import jax.numpy as jnp
from jax import lax
from jax.experimental import pallas as pl
from jax.experimental.pallas import tpu as pltpu
from jax.sharding import PartitionSpec as P

BLOCK = 128
TALL = 64
AHEAD = 2
MESH = pl.DeviceIdType.MESH

decay_rate = 0.95
step_size = 0.3


def slot_table(placement, holders, per_device):
    matches = (placement[:, None, :] == jnp.arange(holders, dtype=jnp.int32)[None, :, None]).astype(
        jnp.int32
    )
    rank_within = jnp.cumsum(matches, axis=-1) - 1
    expert_ids = jnp.arange(placement.shape[-1], dtype=jnp.int32)
    slot_numbers = jnp.arange(per_device, dtype=jnp.int32)
    selected = matches[..., None, :] * (rank_within[..., None, :] == slot_numbers[:, None]).astype(
        jnp.int32
    )
    return jnp.sum(selected * expert_ids, axis=-1)


def route_tables(placement, slots, holders, per_device):
    experts = placement.shape[-1]
    ids = jnp.arange(experts, dtype=jnp.int32)
    needed = jnp.stack(
        [
            jnp.any(placement == 0, axis=0) & (ids >= per_device),
            jnp.any(placement == holders - 1, axis=0) & (ids < experts - per_device),
        ]
    ).astype(jnp.int32)
    rank = jnp.cumsum(needed, axis=-1) - 1
    counts = jnp.sum(needed, axis=-1)
    places = jnp.arange(experts - per_device, dtype=jnp.int32)
    hits = needed[:, None, :] * (rank[:, None, :] == places[None, :, None]).astype(jnp.int32)
    sent = jnp.sum(hits * ids, axis=-1)
    low = jnp.where(ids < per_device, ids, per_device + rank[0])
    high = jnp.where(ids >= experts - per_device, ids, rank[1])
    middle = jnp.broadcast_to(ids, (holders - 2, experts))
    position = jnp.concatenate([low[None], middle, high[None]])
    chosen = (slots[..., None] == ids).astype(jnp.int32)
    read = jnp.sum(chosen * position[None, :, None, :], axis=-1)
    return jnp.concatenate([read.reshape(-1), sent.reshape(-1)]), jnp.max(counts)


def round_heights(rows):
    ramp = [16, 32, 48]
    rest = rows - 2 * sum(ramp)
    if rest >= 0 and rest % TALL == 0:
        return ramp + [TALL] * (rest // TALL) + ramp[::-1]
    return [16] * (rows // 16)


def exchange_kernel(n_rep, n_ep, heights, width, table_ref, w_ref, out_ref, *scratch):
    rounds = len(heights)
    starts = [sum(heights[:t]) for t in range(rounds)]
    lands = scratch[:rounds]
    (stage, packed, own_sem, keep_sem, esend, erecv, zrecv, lsend, rsend, xsend, xrecv) = scratch[
        rounds:
    ]
    z = lax.axis_index("ep")
    me = lax.axis_index("replica")
    per, row_count, _ = w_ref.shape
    goes_left = z >= 2
    goes_right = z <= n_ep - 3
    feeds_end = jnp.logical_or(z == 1, z == n_ep - 2)
    is_end = jnp.logical_or(z == 0, z == n_ep - 1)

    barrier = pltpu.get_barrier_semaphore()
    for step in range(1, n_rep):
        peer = lax.rem(me + step, n_rep)
        pl.semaphore_signal(barrier, inc=1, device_id={"replica": peer}, device_id_type=MESH)

    @pl.when(z > 0)
    def _():
        pl.semaphore_signal(barrier, inc=1, device_id={"ep": z - 1}, device_id_type=MESH)

    @pl.when(z < n_ep - 1)
    def _():
        pl.semaphore_signal(barrier, inc=1, device_id={"ep": z + 1}, device_id_type=MESH)

    def own_copy(t):
        return pltpu.make_async_copy(
            w_ref.at[:, pl.ds(starts[t], heights[t]), :],
            lands[t].at[pl.ds(per * z, per)],
            own_sem.at[t],
        )

    for t in range(rounds):
        own_copy(t).start()

    lines = jnp.where(z > 0, 1, 0) + jnp.where(z < n_ep - 1, 1, 0)
    pl.semaphore_wait(barrier, n_rep - 1 + lines)

    def line_copy(t, q, to, sems):
        piece = lands[t].at[pl.ds(per * q, per)]
        return pltpu.make_async_remote_copy(
            src_ref=piece,
            dst_ref=piece,
            send_sem=sems.at[t, q],
            recv_sem=zrecv.at[t, q],
            device_id={"ep": to},
            device_id_type=MESH,
        )

    def left(t, q):
        return line_copy(t, q, z - 1, lsend)

    def right(t, q):
        return line_copy(t, q, z + 1, rsend)

    def send_left(t, q):
        @pl.when(goes_left)
        def _():
            left(t, q).start()

    def send_right(t, q):
        @pl.when(goes_right)
        def _():
            right(t, q).start()

    def offer(t):
        own_copy(t).wait()
        send_left(t, z)
        send_right(t, z)

    def end_copy(t):
        at_low = z <= 1
        return pltpu.make_async_remote_copy(
            src_ref=packed.at[t % 2, :, pl.ds(0, heights[t]), :],
            dst_ref=lands[t].at[pl.ds(jnp.where(at_low, per, 0), width)],
            send_sem=esend.at[t],
            recv_sem=erecv.at[t],
            device_id={"ep": jnp.where(at_low, 0, n_ep - 1)},
            device_id_type=MESH,
        )

    def rows_of(source, t):
        return pl.ds(pl.multiple_of(source * row_count + starts[t], 16), heights[t])

    def place_copy(t, step):
        return pltpu.make_async_remote_copy(
            src_ref=stage.at[t % 2, step, :, pl.ds(0, heights[t]), :],
            dst_ref=out_ref.at[:, rows_of(me, t), :],
            send_sem=xsend.at[t, step],
            recv_sem=xrecv.at[t, step],
            device_id={"replica": lax.rem(me + step, n_rep)},
            device_id_type=MESH,
        )

    def keep_copy(t):
        return pltpu.make_async_copy(
            stage.at[t % 2, 0, :, pl.ds(0, heights[t]), :],
            out_ref.at[:, rows_of(me, t), :],
            keep_sem.at[t],
        )

    def drain(t):
        keep_copy(t).wait()
        for step in range(1, n_rep):
            place_copy(t, step).wait_send()

    for t in range(min(AHEAD, rounds)):
        offer(t)
    for t in range(rounds):
        if t + AHEAD < rounds:
            offer(t + AHEAD)
        for d in range(1, n_ep):

            @pl.when(jnp.logical_and(z + d < n_ep, z >= 1))
            def _():
                left(t, z + d).wait_recv()
                send_left(t, z + d)

            @pl.when(jnp.logical_and(z - d >= 0, z <= n_ep - 2))
            def _():
                right(t, z - d).wait_recv()
                send_right(t, z - d)

        @pl.when(feeds_end)
        def _():
            if t >= 2:
                end_copy(t - 2).wait_send()
            first = n_rep * n_ep * per + jnp.where(z <= 1, 0, per * (n_ep - 1))
            for i in range(width):
                packed[t % 2, i, : heights[t]] = lands[t][table_ref[first + i]]
            end_copy(t).start()

        @pl.when(is_end)
        def _():
            end_copy(t).wait_recv()

        if t >= 2:
            drain(t - 2)
        for step in list(range(1, n_rep)) + [0]:
            dest = lax.rem(me + step, n_rep)
            for k in range(per):
                slot = table_ref[(dest * n_ep + z) * per + k]
                stage[t % 2, step, k, : heights[t]] = lands[t][slot]
            if step:
                place_copy(t, step).start()
            else:
                keep_copy(t).start()

    for t in range(max(rounds - 2, 0), rounds):
        drain(t)

        @pl.when(feeds_end)
        def _():
            end_copy(t).wait_send()

    for t in range(rounds):
        for step in range(1, n_rep):
            place_copy(t, step).wait_recv()
        for d in range(n_ep):

            @pl.when(jnp.logical_and(z + d < n_ep, goes_left))
            def _():
                left(t, z + d).wait_send()

            @pl.when(jnp.logical_and(z - d >= 0, goes_right))
            def _():
                right(t, z - d).wait_send()


def exchange(table, weights, n_rep, n_ep, width, collective_id):
    per, row_count, col_count = weights.shape
    heights = round_heights(row_count)
    rounds, tallest = len(heights), max(heights)
    dma = pltpu.SemaphoreType.DMA
    moved = 2 * per * n_rep * row_count * col_count * 2
    return pl.pallas_call(
        functools.partial(exchange_kernel, n_rep, n_ep, heights, width),
        out_shape=jax.ShapeDtypeStruct((per, n_rep * row_count, col_count), weights.dtype),
        in_specs=[
            pl.BlockSpec(memory_space=pltpu.SMEM),
            pl.BlockSpec(memory_space=pl.ANY),
        ],
        out_specs=pl.BlockSpec(memory_space=pl.ANY),
        scratch_shapes=[
            pltpu.VMEM((per * n_ep, height, col_count), weights.dtype) for height in heights
        ]
        + [
            pltpu.VMEM((2, n_rep, per, tallest, col_count), weights.dtype),
            pltpu.VMEM((2, width, tallest, col_count), weights.dtype),
            dma((rounds,)),
            dma((rounds,)),
            dma((rounds,)),
            dma((rounds,)),
            dma((rounds, n_ep)),
            dma((rounds, n_ep)),
            dma((rounds, n_ep)),
            dma((rounds, n_rep)),
            dma((rounds, n_rep)),
        ],
        compiler_params=pltpu.CompilerParams(
            collective_id=collective_id, has_side_effects=True, vmem_limit_bytes=54 * 1024 * 1024
        ),
        cost_estimate=pl.CostEstimate(flops=0, bytes_accessed=moved, transcendentals=0),
    )(table, weights)


def total_kernel(axes, x_ref, out_ref, *scratch):
    barrier = pltpu.get_barrier_semaphore()
    for name, size in axes:
        me = lax.axis_index(name)
        for step in range(1, size):
            pl.semaphore_signal(
                barrier,
                inc=1,
                device_id={name: lax.rem(me + step, size)},
                device_id_type=MESH,
            )
    pl.semaphore_wait(barrier, sum(size - 1 for _, size in axes))
    current = x_ref[...]
    for phase, (name, size) in enumerate(axes):
        held, send_sem, recv_sem = scratch[3 * phase : 3 * phase + 3]
        me = lax.axis_index(name)
        held[me] = current
        copies = []
        for step in range(1, size):
            copy = pltpu.make_async_remote_copy(
                src_ref=held.at[me],
                dst_ref=held.at[me],
                send_sem=send_sem.at[step],
                recv_sem=recv_sem.at[step],
                device_id={name: lax.rem(me + step, size)},
                device_id_type=MESH,
            )
            copy.start()
            copies.append(copy)
        for copy in copies:
            copy.wait()
        current = held[0]
        for index in range(1, size):
            current = current + held[index]
    out_ref[...] = current


def total(value, axes, collective_id):
    scratch = []
    for _, size in axes:
        scratch += [
            pltpu.VMEM((size, 8, 128), jnp.float32),
            pltpu.SemaphoreType.DMA((size,)),
            pltpu.SemaphoreType.DMA((size,)),
        ]
    summed = pl.pallas_call(
        functools.partial(total_kernel, axes),
        out_shape=jax.ShapeDtypeStruct((8, 128), jnp.float32),
        in_specs=[pl.BlockSpec(memory_space=pltpu.VMEM)],
        out_specs=pl.BlockSpec(memory_space=pltpu.VMEM),
        scratch_shapes=scratch,
        compiler_params=pltpu.CompilerParams(collective_id=collective_id, has_side_effects=True),
    )(jnp.broadcast_to(value, (8, 128)))
    return summed[0, 0]


def scale_kernel(w_ref, out_ref, scale_ref):
    cells = w_ref.shape[2] // BLOCK
    lane = lax.broadcasted_iota(jnp.int32, (1, cells), 1)
    for strip in range(w_ref.shape[1] // BLOCK):
        rows = slice(strip * BLOCK, (strip + 1) * BLOCK)
        peaks = []
        for cell in range(cells):
            columns = slice(cell * BLOCK, (cell + 1) * BLOCK)
            sizes = jnp.abs(w_ref[0, rows, columns]).reshape(BLOCK // 16, 16, BLOCK)
            column_peaks = jnp.max(jnp.max(sizes, axis=0).astype(jnp.float32), axis=0, keepdims=True)
            peaks.append(jnp.max(column_peaks, axis=1, keepdims=True) + 1e-06)
        scales = jnp.zeros((1, cells), jnp.float32)
        for cell, largest in enumerate(peaks):
            columns = slice(cell * BLOCK, (cell + 1) * BLOCK)
            values = w_ref[0, rows, columns].astype(jnp.float32)
            out_ref[0, rows, columns] = (values * (1.0 / largest)).astype(out_ref.dtype)
            scales = jnp.where(lane == cell, largest, scales)
        scale_ref[0, strip] = scales


def block_quantize(weights):
    per, row_count, col_count = weights.shape
    strips, cells = row_count // BLOCK, col_count // BLOCK
    group = 2 if strips % 2 == 0 else 1
    scaled, scales = pl.pallas_call(
        scale_kernel,
        grid=(per, strips // group),
        in_specs=[pl.BlockSpec((1, group * BLOCK, col_count), lambda k, i: (k, i, 0))],
        out_specs=[
            pl.BlockSpec((1, group * BLOCK, col_count), lambda k, i: (k, i, 0)),
            pl.BlockSpec((1, group, 1, cells), lambda k, i: (k, i, 0, 0)),
        ],
        out_shape=[
            jax.ShapeDtypeStruct(weights.shape, weights.dtype),
            jax.ShapeDtypeStruct((per, strips, 1, cells), jnp.float32),
        ],
        compiler_params=pltpu.CompilerParams(vmem_limit_bytes=32 * 1024 * 1024),
    )(weights)
    return scaled, scales[:, :, 0]


def body(master, gradient, second, placement):
    values = gradient.astype(jnp.float32)
    n_train = lax.axis_size("train")
    n_rep = lax.axis_size("replica")
    n_ep = lax.axis_size("ep")
    axes = (("train", n_train), ("replica", n_rep), ("ep", n_ep))
    square_sum = total(jnp.sum(values * values), axes, 0)
    root_mean = jnp.sqrt(square_sum / (values.size * n_train * n_rep * n_ep) + 1e-06)
    clipped = values / root_mean
    second_new = decay_rate * second + (1.0 - decay_rate) * clipped * clipped
    master_new = master - step_size * clipped / (jnp.sqrt(second_new) + 1e-08)
    weights = master_new.astype(jnp.bfloat16)
    per = weights.shape[0]
    table, most = route_tables(placement, slot_table(placement, n_ep, per), n_ep, per)
    widths = list(range(per * (n_ep - 2), per * (n_ep - 1) + 1))

    def at_width(index, width):
        def run(operands):
            return block_quantize(exchange(*operands, n_rep, n_ep, width, 1 + index))

        return run

    scaled, scales = lax.switch(
        jnp.clip(most - widths[0], 0, len(widths) - 1),
        [at_width(index, width) for index, width in enumerate(widths)],
        (table, weights),
    )
    return (master_new, second_new, scaled[None, None], scales[None, None])


def solution(mesh):
    return jax.shard_map(
        body,
        mesh=mesh,
        in_specs=(
            P("ep", "replica", "train"),
            P("ep", "replica", "train"),
            P("ep", "replica", "train"),
            P(),
        ),
        out_specs=(
            P("ep", "replica", "train"),
            P("ep", "replica", "train"),
            P("replica", "ep", None, None, "train"),
            P("replica", "ep", None, None, "train"),
        ),
        check_vma=False,
    )
```

time: 635 us -> 525 us (0.83)
  Pallas kernels: 556 us -> 485 us
  blocking collectives: 42.2 us -> 0 us
    pallas_call x2 -> x3, Pallas kernels: 556 us -> 485 us  [the longest x1 439 us: exchange(): pl.pallas_call(functools.partial(exchange_kernel, n_rep, n_ep, heights, w...]
    psum x1 -> x0, blocking collectives: 42.2 us -> none  [body(): square_sum = lax.psum(jnp.sum(values * values), ('train', 'replica', 'ep'))]
where the time goes in v2:
time: 525 us; the launch traced here: 523 us
  Pallas kernels  485 us (92%)
  other arithmetic  33.7 us (6%)
    pallas_call x1, Pallas kernels, exchange(): pl.pallas_call(functools.partial(exchange_kernel, n_rep, n_ep, heights, w...  439 us
    pallas_call x1, Pallas kernels, block_quantize(): pl.pallas_call(scale_kernel, grid=(per, strips // group), in_specs=[pl.Bl...  30.5 us
    convert_element_type x1, other arithmetic, body(): weights = master_new.astype(jnp.bfloat16)  22.3 us
    pallas_call x1, Pallas kernels, total(): pl.pallas_call(functools.partial(total_kernel, axes), out_shape=jax.Shape...  14.9 us

profile of v2, /device:TPU:0, one launch (start us, length us, event | category | flops | bytes accessed | tf_op | source)
XLA Modules:
  0.0 523.1 jit_solution(16458999588357946000)
XLA Ops:
  0.6 7.5 %fusion = f32[]{:T(128)} fusion(bf16[2,512,3584]{2,1,0:T(8,128)(2,1)} %param.8), kind=kLoop, calls=%fused_computation.3 | loop fusion | flops 11010047 | bytes 7340036 | tf_op jit(solution)/shard_map/reduce_sum | solution.py:375
  8.1 0.7 compare_reduce_fusion.1
  8.8 0.1 fusion.5
  8.9 0.6 reduce_max.9
  10.2 0.2 reduce_window_sum.23
  10.5 0.2 fusion.4
  10.6 0.1 copy.9
  10.7 0.1 reshape.103
  10.8 1.2 broadcast_in_dim.15.x_ref
  12.1 14.9 %shard_map.75 = f32[8,128]{1,0:T(8,128)} custom-call(f32[8,128]{1,0:T(8,128)} %broadcast_in_dim.15.x_ref), custom_call_target="tpu_custom_call" | custom-call | tf_op jit(solution)/shard_map/pallas_call | solution.py:317
  27.0 1.2 slice.9
  28.8 0.7 fusion.2
  29.5 0.7 reduce_window_sum.22
  30.3 0.2 multiply_reduce_fusion
  30.5 0.3 select_reduce_fusion
  30.8 0.1 copy.8
  30.9 0.1 reshape.102
  31.0 0.1 pad_add_fusion.1
  31.1 22.3 %fusion.6 = (bf16[2,512,3584]{2,1,0:T(8,128)(2,1)S(1)}, f32[2,512,3584]{2,1,0:T(8,128)}, f32[2,512,3584]{2,1,0:T(8,128)}) fusion(f32[2,512,3584]{2,1,0:T(8,128)} %param.7, f32[]{:T(128)} %bitcast.3, bf16[2,512,3584]{2,1,0:T(8,128)(2,1)} %param.8, f32[2,512,3584]{2,1,0:T(8,128)} %param.9), kind=kLoop, calls=%fused_computation.27 | loop fusion | flops 40370176 | bytes 73400320 | tf_op jit(solution)/shard_map/convert_element_type | solution.py:380
  53.4 469.7 %conditional.1 = (bf16[2,2048,3584]{2,1,0:T(8,128)(2,1)}, f32[1,1,2,16,28]{4,3,2,1,0:T(8,128)}) conditional(s32[]{:T(128)} %clamp.3, (s32[44]{0:T(128)S(1)}, bf16[2,512,3584]{2,1,0:T(8,128)(2,1)S(1)}) %tuple.23, (s32[44]{0:T(128)S(1)}, bf16[2,512,3584]{2,1,0:T(8,128)(2,1)S(1)}) %tuple.23, (s32[44]{0:T(128)S(1)}, ...), branch_computations={%region_10.11_spmd, %region_11.12_spmd, %region_12.13_spmd} | conditional | bytes 58720272 | solution.py:391
  53.4 439.2 %branch_0_fun.2.w_ref = bf16[2,2048,3584]{2,1,0:T(8,128)(2,1)} custom-call(s32[44]{0:T(128)S(1)} %get-tuple-element.13.table_ref, bf16[2,512,3584]{2,1,0:T(8,128)(2,1)S(1)} %get-tuple-element.14.w_ref), custom_call_target="tpu_custom_call" | custom-call | bytes 58720256 | tf_op jit(solution)/shard_map/cond/branch_0_fun/pallas_call | solution.py:241
  492.6 30.5 %branch_0_fun.3 = (bf16[2,2048,3584]{2,1,0:T(8,128)(2,1)}, f32[2,16,1,28]{3,2,1,0:T(1,128)}) custom-call(bf16[2,2048,3584]{2,1,0:T(8,128)(2,1)} %branch_0_fun.2.w_ref), custom_call_target="tpu_custom_call" | custom-call | tf_op jit(solution)/shard_map/cond/branch_0_fun/pallas_call | solution.py:352
  (7 shorter events, 0.1 us)
